TPU v7x, 32 devices: a whole 2x2x4 slice. The times are simulated.
32 devices in a mesh: tile: 8 (over z, y), rank: 4 (over x, core).
Axes of the slice: x: 2, y: 2, z: 4, core: 2. Of those that a mesh axis runs over, the one named last changes fastest.
Arguments:
- step_now: float32 [65536], P(('tile', 'rank')), may hold values from -6 to 6
- residual: float32 [65536], P(('tile', 'rank')), may hold values from -20 to 20
- direction: float32 [65536], P(('tile', 'rank')), may hold values from -20 to 20
- slab_perm: int32 [65536], P(('tile', 'rank')), may hold values from 0 to 2047, as said below
- col_basis: bfloat16 [64, 65536], P(None, ('tile', 'rank')), may hold values from -0.0625 to 0.0625
- row_basis: bfloat16 [64, 6, 32768], P(None, None, ('tile', 'rank')), may hold values from -0.75 to 0.75
- coupling: bfloat16 [8, 8, 64, 64], P('tile'), may hold values from -0.375 to 0.375
- near_blocks: bfloat16 [640, 6, 64, 128], P(('tile', 'rank')), may hold values from -0.5 to 0.5
- near_leaf: int32 [640], P(('tile', 'rank')), may hold values from 0 to 15
- near_target: int32 [640], P(('tile', 'rank')), may hold values from 0 to 191, as said below
- near_live: int32 [32], P(('tile', 'rank')), may hold values from 3 to 20, as said below
- data_weight: float32 [6, 32768], P(None, ('tile', 'rank')), may hold values from 0.25 to 4
Outputs:
- new_step: float32 [65536], P(('tile', 'rank'))
- new_residual: float32 [65536], P(('tile', 'rank'))
- new_direction: float32 [65536], P(('tile', 'rank'))
Inputs may be any that keep to these rules, and one draw needn't show every extreme that they name: `slab_perm`: each device's block of 2048 consecutive entries is a permutation of 0 to 2047. The tile offset near_target[g] // 64 is 0, 1 or 2; on every device the first three slots take the offsets 0, 1 and 2 in some order. The first near_live[d] of device d's 20 slots are live.
All inputs are finite; a program needn't handle non-finite values.
Results may differ from a plain program's by a relative error of at most 0.007.
Values may be sent and summed in bfloat16 or wider, within the bound.
A program may use at most 64 MiB of HBM per device.

v0:
```python
import jax
import jax.numpy as jnp
from jax import lax
from jax.sharding import PartitionSpec as P

LEAF = 128
LD = 64


damping_weight = 0.5
tiny_value = 1e-06


def with_halo(block, sides, width):
    for axis, dim in sides:
        count = lax.axis_size(axis)
        forward = [(i, i + 1) for i in range(count - 1)]
        backward = [(target, source) for source, target in forward]
        low = lax.ppermute(
            lax.slice_in_dim(block, block.shape[dim] - width, None, axis=dim), axis, forward
        )
        high = lax.ppermute(lax.slice_in_dim(block, 0, width, axis=dim), axis, backward)
        block = jnp.concatenate([low, block, high], axis=dim)
    return block


def per_device(
    step_now,
    residual,
    direction,
    slab_perm,
    col_basis,
    row_basis,
    coupling,
    near_blocks,
    near_leaf,
    near_target,
    near_live,
    data_weight,
):
    tile_count = lax.axis_size("tile")
    rank_count = lax.axis_size("rank")
    tile_here = lax.axis_index("tile")
    slab_len = direction.shape[0]
    piece_len = slab_len // tile_count
    tile_points = data_weight.shape[1] * rank_count
    data_leaves = tile_points // LD
    leaf_count = slab_len // LEAF
    width_rank = col_basis.shape[0]
    block_slots = near_blocks.shape[0]
    dir_bf = direction.astype(jnp.bfloat16)
    outgoing = dir_bf[slab_perm].reshape(tile_count, piece_len)
    cluster_vec = lax.all_to_all(outgoing, "tile", split_axis=0, concat_axis=0, tiled=True).reshape(
        slab_len
    )
    coef_part = jnp.dot(col_basis, cluster_vec, preferred_element_type=jnp.float32)
    coef_all = lax.all_gather(coef_part[None, :], ("tile", "rank"), axis=0, tiled=True)
    cluster_coef = (
        coef_all.reshape(tile_count, rank_count, width_rank).sum(axis=1).astype(jnp.bfloat16)
    )
    far_keep = jnp.abs(jnp.arange(tile_count, dtype=jnp.int32) - tile_here) > 1
    masked_coef = cluster_coef * far_keep[:, None].astype(jnp.bfloat16)
    far_coef = jnp.einsum(
        "cab,cb->a", coupling[0], masked_coef, preferred_element_type=jnp.float32
    ).astype(jnp.bfloat16)
    basis_flat = row_basis.reshape(width_rank, -1)
    far_data = jnp.dot(far_coef, basis_flat, preferred_element_type=jnp.float32).reshape(6, -1)
    live_mask = jnp.arange(block_slots, dtype=jnp.int32) < near_live[0]
    offset = near_target // data_leaves
    data_leaf = near_target % data_leaves
    picked = cluster_vec.reshape(leaf_count, LEAF)[near_leaf]
    values = jnp.einsum("bkij,bj->bki", near_blocks, picked, preferred_element_type=jnp.float32)
    values = values * live_mask[:, None, None].astype(jnp.float32)
    partial_value = (
        jnp.zeros((3, 6, data_leaves, LD), jnp.float32).at[offset, :, data_leaf, :].add(values)
    )
    partial_value = partial_value.reshape(3, 6, tile_points)
    shares = lax.psum_scatter(partial_value, "rank", scatter_dimension=2, tiled=True)
    edges = jnp.stack([shares[0], shares[2]])
    extended = with_halo(edges, (("tile", 0),), 1)
    near_data = shares[1] + extended[0] + extended[3]
    weighted = (data_weight * (far_data + near_data)).astype(jnp.bfloat16)
    back_part = jnp.dot(basis_flat, weighted.reshape(-1), preferred_element_type=jnp.float32)
    back_coef = lax.psum(back_part, "rank").astype(jnp.bfloat16)
    spread = jnp.einsum("cab,a->cb", coupling[0], back_coef, preferred_element_type=jnp.float32)
    spread = spread * far_keep[:, None].astype(jnp.float32)
    cluster_back = lax.psum_scatter(spread, "tile", scatter_dimension=0, tiled=True).astype(
        jnp.bfloat16
    )
    far_back = jnp.dot(cluster_back[0], col_basis, preferred_element_type=jnp.float32)
    tile_data = lax.all_gather(weighted, "rank", axis=1, tiled=True)
    window = with_halo(tile_data[None], (("tile", 0),), 1)
    chosen = window.reshape(3, 6, data_leaves, LD)[offset, :, data_leaf, :]
    back_values = jnp.einsum(
        "bkij,bki->bj", near_blocks, chosen, preferred_element_type=jnp.float32
    )
    back_values = back_values * live_mask[:, None].astype(jnp.float32)
    near_back = (
        jnp.zeros((leaf_count, LEAF), jnp.float32).at[near_leaf].add(back_values).reshape(slab_len)
    )
    cluster_image = far_back + near_back
    returned = lax.all_to_all(
        cluster_image.reshape(tile_count, piece_len),
        "tile",
        split_axis=0,
        concat_axis=0,
        tiled=True,
    ).reshape(slab_len)
    slab_image = jnp.zeros((slab_len,), jnp.float32).at[slab_perm].set(returned)
    normal_image = slab_image + damping_weight * direction
    norm_now, curvature = lax.psum(
        (jnp.sum(residual * residual), jnp.sum(direction * normal_image)), ("tile", "rank")
    )
    norm_now = norm_now + tiny_value
    step_size = norm_now / (curvature + tiny_value)
    new_step = step_now + step_size * direction
    new_residual = residual - step_size * normal_image
    norm_next = lax.psum(jnp.sum(new_residual * new_residual), ("tile", "rank"))
    new_direction = new_residual + norm_next / norm_now * direction
    return (new_step, new_residual, new_direction)


def solution(mesh):
    return jax.shard_map(
        per_device,
        mesh=mesh,
        in_specs=(
            P(("tile", "rank")),
            P(("tile", "rank")),
            P(("tile", "rank")),
            P(("tile", "rank")),
            P(None, ("tile", "rank")),
            P(None, None, ("tile", "rank")),
            P("tile", None, None, None),
            P(("tile", "rank"), None, None, None),
            P(("tile", "rank")),
            P(("tile", "rank")),
            P(("tile", "rank")),
            P(None, ("tile", "rank")),
        ),
        out_specs=(P(("tile", "rank")), P(("tile", "rank")), P(("tile", "rank"))),
        check_vma=False,
    )
```

profile of v0, /device:TPU:0, one launch (start us, length us, event | category | flops | bytes accessed | tf_op | source)
XLA Modules:
  0.0 243.1 jit_solution(3129177111253326644)
XLA Ops:
  7.2 0.8 broadcast_clamp_fusion
  8.0 0.7 convert_element_type.48
  8.7 13.1 %gather_fusion = bf16[2048]{0:T(1024)(128)(2,1)S(1)} fusion(bf16[2048]{0:T(1024)(128)(2,1)S(1)} %convert_element_type.48, s32[2048]{0:T(1024)S(1)} %get-tuple-element.11), kind=kCustom, calls=%fused_computation | custom fusion | bytes 16384 | tf_op jit(solution)/shard_map/gather | solution.py:52
  22.3 0.7 reduce.1
  23.0 0.6 reshape.150
  23.6 7.3 %all-to-all-start = ((bf16[8,2,128]{2,1,0:T(2,128)(2,1)}), bf16[8,2,128]{2,1,0:T(2,128)(2,1)S(1)}, u32[]{:S(2)}, u32[]{:S(2)}) async-start(bf16[8,2,128]{2,1,0:T(2,128)(2,1)} %reshape.150), calls=%async_computation | async-start | bytes 8192 | tf_op jit(solution)/shard_map/all_to_all | solution.py:53
  31.7 5.6 %all-to-all-done = bf16[8,2,128]{2,1,0:T(2,128)(2,1)S(1)} async-done(((bf16[8,2,128]{2,1,0:T(2,128)(2,1)}), bf16[8,2,128]{2,1,0:T(2,128)(2,1)S(1)}, u32[]{:S(2)}, u32[]{:S(2)}) %all-to-all-start) | async-done | bytes 4128 | tf_op jit(solution)/shard_map/all_to_all | solution.py:53
  37.9 1.6 fusion.19
  39.7 2.1 scatter_fusion
  42.0 0.9 reshape.72
  43.5 1.1 convolution_bitcast_fusion.2
  44.9 38.4 %all-reduce = f32[2048]{0:T(1024)S(1)} all-reduce(f32[2048]{0:T(1024)S(1)} %dynamic-update-slice), channel_id=2, replica_groups=mesh['tile'=8,'rank'=4] {'tile','rank'}, use_global_device_ids=true, to_apply=%add | all-reduce | flops 2048 | bytes 16384
  83.4 0.8 fusion.38
  84.2 1.3 collective-permute-start.1
  85.5 4.8 %collective-permute-start = (f32[1,6,1024]{2,1,0:T(8,128)S(1)}, f32[1,6,1024]{2,1,0:T(8,128)S(1)}, u32[]{:S(2)}, u32[]{:S(2)}) collective-permute-start(f32[1,6,1024]{2,1,0:T(8,128)S(1)} %get-tuple-element.7), channel_id=1, source_target_pairs={{0,4},{4,8},{8,12},{12,16},{16,20},{20,24},{24,28},{1,5},{5,9},{9,... | collective-permute-start | bytes 73736 | tf_op jit(solution)/shard_map/ppermute | solution.py:19
  90.3 1.6 fusion.2
  92.0 0.8 fusion.15
  92.7 5.2 %all_gather.7 = bf16[6,4096]{1,0:T(8,128)(2,1)S(1)} all-gather(bf16[6,1024]{1,0:T(8,128)(2,1)S(1)} %fusion.15), channel_id=1, replica_groups=mesh['tile'=8,'rank'=4] {'rank'}, dimensions={1}, use_global_device_ids=true | all-gather | bytes 61440 | tf_op jit(solution)/shard_map/all_gather | solution.py:91
  98.0 1.3 collective-permute-start.3
  99.3 5.5 %collective-permute-start.2 = (bf16[1,6,4096]{2,1,0:T(8,128)(2,1)S(1)}, bf16[1,6,4096]{2,1,0:T(8,128)(2,1)S(1)}, u32[]{:S(2)}, u32[]{:S(2)}) collective-permute-start(bf16[1,6,4096]{2,1,0:T(8,128)(2,1)S(1)} %bitcast.109), channel_id=1, source_target_pairs={{0,4},{4,8},{8,12},{12,16},{16,20},{20,24},{24,28},{1,5},{5,9},{9,... | collective-permute-start | bytes 147464 | tf_op jit(solution)/shard_map/ppermute | solution.py:19
  105.1 6.8 %psum.29 = bf16[64]{0:T(256)(128)(2,1)S(1)} all-reduce(f32[64]{0:T(128)S(1)} %convolution_bitcast_fusion), channel_id=1, replica_groups=mesh['tile'=8,'rank'=4] {'rank'}, use_global_device_ids=true, to_apply=%region_5.6 | all-reduce | flops 64 | bytes 384 | tf_op jit(solution)/shard_map/psum | solution.py:84
  112.1 20.9 %all-reduce.1 = bf16[8,64]{1,0:T(8,128)(2,1)S(1)} all-reduce(f32[8,64]{1,0:T(8,128)S(1)} %broadcast_multiply_fusion), channel_id=4, replica_groups=mesh['tile'=8,'rank'=4] {'tile'}, use_global_device_ids=true, to_apply=%region_6.7.clone | all-reduce | flops 512 | bytes 3072
  132.9 0.8 fusion.31
  134.5 0.7 gather_fusion.2
  135.7 0.7 scatter_custom_fusion.1
  136.5 8.9 %all_to_all.19 = f32[8,1,256]{2,1,0:T(1,128)S(1)} all-to-all(f32[8,1,256]{2,1,0:T(1,128)S(1)} %bitcast.114), channel_id=1, replica_groups=mesh['tile'=8,'rank'=4] {'tile'}, dimensions={0} | all-to-all | bytes 16384 | tf_op jit(solution)/shard_map/all_to_all | solution.py:102
  145.4 8.0 %scatter_custom_fusion.2 = f32[2048]{0:T(1024)S(1)} fusion(s32[2048]{0:T(1024)S(1)} %get-tuple-element.12, f32[2048]{0:T(1024)S(1)} %bitcast.117, f32[]{:T(128)} %constant.20.clone.1), kind=kCustom, calls=%fused_computation.47 | custom fusion | bytes 8196 | tf_op jit(solution)/shard_map/scatter | solution.py:109
  153.4 0.6 multiply_reduce_fusion.1
  154.0 38.5 %all-reduce.2 = (f32[]{:T(128)}, f32[]{:T(128)}) all-reduce(f32[]{:T(128)} %get-tuple-element.16, f32[]{:T(128)} %get-tuple-element.15), channel_id=1, replica_groups=mesh['tile'=8,'rank'=4] {'tile','rank'}, use_global_device_ids=true, to_apply=%region_1.2 | all-reduce | flops 2 | bytes 16 | tf_op jit(solution)/shard_map/psum | solution.py:111
  193.8 0.6 multiply_reduce_fusion
  194.5 40.5 %psum.31 = f32[]{:T(128)} all-reduce(f32[]{:T(128)} %get-tuple-element.5), channel_id=1, replica_groups=mesh['tile'=8,'rank'=4] {'tile','rank'}, use_global_device_ids=true, to_apply=%region_12.13 | all-reduce | flops 1 | bytes 8 | tf_op jit(solution)/shard_map/psum | solution.py:118
  235.7 0.6 multiply_add_fusion
  (64 shorter events, 4.3 us)
Async XLA Ops:
  7.2 30.8 %copy-start = (bf16[20,6,64,128]{3,2,1,0:T(8,128)(2,1)S(1)}, bf16[20,6,64,128]{3,2,1,0:T(8,128)(2,1)}, u32[]{:S(2)}) copy-start(bf16[20,6,64,128]{3,2,1,0:T(8,128)(2,1)} %param.19) | copy-start | bytes 5898244
  8.7 22.2 %copy-start.9 = (s32[20]{0:T(128)S(1)}, s32[20]{0:T(128)}, u32[]{:S(2)}) copy-start(s32[20]{0:T(128)} %param.21) | copy-start | bytes 244
  8.7 22.3 %copy-start.10 = (s32[20]{0:T(128)S(1)}, s32[20]{0:T(128)}, u32[]{:S(2)}) copy-start(s32[20]{0:T(128)} %param.20) | copy-start | bytes 244
  23.6 13.7 %all-to-all-start = ((bf16[8,2,128]{2,1,0:T(2,128)(2,1)}), bf16[8,2,128]{2,1,0:T(2,128)(2,1)S(1)}, u32[]{:S(2)}, u32[]{:S(2)}) async-start(bf16[8,2,128]{2,1,0:T(2,128)(2,1)} %reshape.150), calls=%async_computation | async-start | bytes 8192 | tf_op jit(solution)/shard_map/all_to_all | solution.py:53
  30.9 52.5 %reduce-scatter.2.cloned.1.call-start = ((), (), s32[]{:S(2)}) async-start(), calls=%async_computation.3 | async-start | bytes 491520 | tf_op jit(solution)/shard_map/reduce_scatter | solution.py:78
  39.5 3.4 %copy-start.11 = (u32[32]{0:T(128)S(1)}, u32[32]{0:T(128)}, u32[]{:S(2)}) copy-start(u32[32]{0:T(128)} %constant.93) | copy-start | bytes 388
  41.8 50.1 %copy-start.5 = (f32[6,1024]{1,0:T(8,128)S(1)}, f32[6,1024]{1,0:T(8,128)}, u32[]{:S(2)}) copy-start(f32[6,1024]{1,0:T(8,128)} %param.23) | copy-start | bytes 73732
  41.9 69.9 %copy-start.2 = (bf16[1,8,64,64]{3,2,1,0:T(8,128)(2,1)S(1)}, bf16[1,8,64,64]{3,2,1,0:T(8,128)(2,1)}, u32[]{:S(2)}) copy-start(bf16[1,8,64,64]{3,2,1,0:T(8,128)(2,1)} %param.18) | copy-start | bytes 196612
  41.9 91.0 %copy-start.1 = (bf16[64,2048]{1,0:T(8,128)(2,1)S(1)}, bf16[64,2048]{1,0:T(8,128)(2,1)}, u32[]{:S(2)}) copy-start(bf16[64,2048]{1,0:T(8,128)(2,1)} %param.16) | copy-start | bytes 786436
  42.9 61.8 %copy-start.8 = (bf16[64,6,1024]{2,0,1:T(8,128)(2,1)S(1)}, bf16[64,6,1024]{2,0,1:T(8,128)(2,1)}, u32[]{:S(2)}) copy-start(bf16[64,6,1024]{2,0,1:T(8,128)(2,1)} %param.17) | copy-start | bytes 2359300
  84.2 7.7 %collective-permute-start.1 = (f32[1,6,1024]{2,1,0:T(8,128)S(1)}, f32[1,6,1024]{2,1,0:T(8,128)S(1)}, u32[]{:S(2)}, u32[]{:S(2)}) collective-permute-start(f32[1,6,1024]{2,1,0:T(8,128)S(1)} %get-tuple-element.8), channel_id=1, source_target_pairs={{4,0},{8,4},{12,8},{16,12},{20,16},{24,20},{28,24},{5,1},{9,5},{13... | collective-permute-start | bytes 73736 | tf_op jit(solution)/shard_map/ppermute | solution.py:22
  85.5 6.5 %collective-permute-start = (f32[1,6,1024]{2,1,0:T(8,128)S(1)}, f32[1,6,1024]{2,1,0:T(8,128)S(1)}, u32[]{:S(2)}, u32[]{:S(2)}) collective-permute-start(f32[1,6,1024]{2,1,0:T(8,128)S(1)} %get-tuple-element.7), channel_id=1, source_target_pairs={{0,4},{4,8},{8,12},{12,16},{16,20},{20,24},{24,28},{1,5},{5,9},{9,... | collective-permute-start | bytes 73736 | tf_op jit(solution)/shard_map/ppermute | solution.py:19
  98.0 36.0 %collective-permute-start.3 = (bf16[1,6,4096]{2,1,0:T(8,128)(2,1)S(1)}, bf16[1,6,4096]{2,1,0:T(8,128)(2,1)S(1)}, u32[]{:S(2)}, u32[]{:S(2)}) collective-permute-start(bf16[1,6,4096]{2,1,0:T(8,128)(2,1)S(1)} %bitcast.108), channel_id=1, source_target_pairs={{4,0},{8,4},{12,8},{16,12},{20,16},{24,20},{28,24},{5,1},{9,5},{13... | collective-permute-start | bytes 147464 | tf_op jit(solution)/shard_map/ppermute | solution.py:22
  99.3 34.9 %collective-permute-start.2 = (bf16[1,6,4096]{2,1,0:T(8,128)(2,1)S(1)}, bf16[1,6,4096]{2,1,0:T(8,128)(2,1)S(1)}, u32[]{:S(2)}, u32[]{:S(2)}) collective-permute-start(bf16[1,6,4096]{2,1,0:T(8,128)(2,1)S(1)} %bitcast.109), channel_id=1, source_target_pairs={{0,4},{4,8},{8,12},{12,16},{16,20},{20,24},{24,28},{1,5},{5,9},{9,... | collective-permute-start | bytes 147464 | tf_op jit(solution)/shard_map/ppermute | solution.py:19
  133.9 19.5 %copy-start.3 = (f32[2048]{0:T(1024)S(1)}, f32[2048]{0:T(1024)}, u32[]{:S(2)}) copy-start(f32[2048]{0:T(1024)} %param.14) | copy-start | bytes 24580
  133.9 19.5 %copy-start.4 = (f32[2048]{0:T(1024)S(1)}, f32[2048]{0:T(1024)}, u32[]{:S(2)}) copy-start(f32[2048]{0:T(1024)} %param.13) | copy-start | bytes 24580
  133.9 101.7 %copy-start.7 = (f32[2048]{0:T(1024)S(1)}, f32[2048]{0:T(1024)}, u32[]{:S(2)}) copy-start(f32[2048]{0:T(1024)} %param.12) | copy-start | bytes 24580
  194.4 41.8 %copy-start.6 = (f32[2048]{0:T(1024)}, f32[2048]{0:T(1024)S(1)}, u32[]{:S(2)}) copy-start(f32[2048]{0:T(1024)S(1)} %get-tuple-element.6) | copy-start | bytes 24580
Sparse Core Ops, SparseCore 0:
  43.0 18.1 reduce-scatter.1
where the time goes:
time: 244 us; the launch traced here: 243 us
  blocking collectives  159 us (65%)
  local copies, waits for them, and re-layouts  26.9 us (11%)
  starting transfers between devices  20.1 us (8%)
  between operations  17 us (7%)
  other arithmetic  8.11 us (3%)
  matrix products  6.13 us (3%)
  waiting for transfers between devices  5.65 us (2%)
    unnamed x2, blocking collectives  59.2 us
    psum x1, blocking collectives, per_device(): norm_next = lax.psum(jnp.sum(new_residual * new_residual), ('tile', 'rank'))  40.5 us
    psum x1, blocking collectives, per_device(): lax.psum((jnp.sum(residual * residual), jnp.sum(direction * normal_image)...  38.5 us
    gather x1, local copies, waits for them, and re-layouts, per_device(): outgoing = dir_bf[slab_perm].reshape(tile_count, piece_len)  13.1 us
    ppermute x2, starting transfers between devices, with_halo(): lax.ppermute(lax.slice_in_dim(block, block.shape[dim] - width, None, axis...  10.3 us
    all_to_all x1, blocking collectives, per_device(): lax.all_to_all(cluster_image.reshape(tile_count, piece_len), 'tile', spli...  8.88 us
    scatter x1, local copies, waits for them, and re-layouts, per_device(): slab_image = jnp.zeros((slab_len,), jnp.float32).at[slab_perm].set(returned)  8.05 us
    all_to_all x1, starting transfers between devices, per_device(): lax.all_to_all(outgoing, 'tile', split_axis=0, concat_axis=0, tiled=True)  7.28 us
  transfers between devices with their start and end apart: 6, of which 1 were waited for; matrix products, arithmetic and copies ran while one was open for 2% of the time, Pallas kernels for 0%

commit v1 on v0

--- a/solution.py
+++ b/solution.py
@@ -1,6 +1,10 @@
+import functools
+
 import jax
 import jax.numpy as jnp
 from jax import lax
+from jax.experimental import pallas as pl
+from jax.experimental.pallas import tpu as pltpu
 from jax.sharding import PartitionSpec as P
 
 LEAF = 128
@@ -120,9 +124,553 @@
     return (new_step, new_residual, new_direction)
 
 
+def split_bf16(x, parts):
+    out = []
+    for _ in range(parts):
+        head = x.astype(jnp.bfloat16)
+        out.append(head)
+        x = x - head.astype(jnp.float32)
+    return out
+
+
+def dot_nt(a, b):
+    return lax.dot_general(a, b, (((1,), (1,)), ((), ())), preferred_element_type=jnp.float32)
+
+
+def dot_nn(a, b):
+    return jnp.dot(a, b, preferred_element_type=jnp.float32)
+
+
+def iota(shape, dim):
+    return lax.broadcasted_iota(jnp.int32, shape, dim)
+
+
+def cg_kernel(
+    dims,
+    residual_ref,
+    direction_ref,
+    perm_ref,
+    col_hbm,
+    row_hbm,
+    coupling_hbm,
+    blocks_hbm,
+    leaf_ref,
+    target_ref,
+    live_ref,
+    weight_ref,
+    image_out,
+    alpha_out,
+    beta_out,
+    col_ref,
+    row_ref,
+    coupling_ref,
+    blocks_ref,
+    onehot_ref,
+    slots_ref,
+    weight_s,
+    far_s,
+    weighted_f,
+    a_send,
+    a_recv,
+    vec_f,
+    res_f,
+    b_send,
+    b_recv,
+    c_send,
+    c_recv,
+    d_send,
+    d_recv,
+    e_send,
+    e_recv,
+    far_back_s,
+    image_s,
+    f_recv,
+    g_send,
+    g_recv,
+    values_s,
+    load_sem,
+    a_ss,
+    a_rs,
+    b_ss,
+    b_rs,
+    c_ss,
+    c_rs,
+    d_ss,
+    d_rs,
+    e_ss,
+    e_rs,
+    f_ss,
+    f_rs,
+    g_ss,
+    g_rs,
+):
+    T, RK, NBS, KC, WR = dims
+    bf16, f32 = jnp.bfloat16, jnp.float32
+    rows = direction_ref.shape[0]
+    pr = rows // T
+    G = weight_ref.shape[1] // 128
+    KG = KC * G
+    gt = G * RK
+    NBP = values_s.shape[0]
+    KI = KC * LD
+    t = lax.axis_index("tile")
+    r = lax.axis_index("rank")
+    me = t * RK + r
+
+    def remote(src, dst, ss, rs, tile, rank):
+        return pltpu.make_async_remote_copy(
+            src_ref=src,
+            dst_ref=dst,
+            send_sem=ss,
+            recv_sem=rs,
+            device_id=(tile, rank),
+            device_id_type=pl.DeviceIdType.MESH,
+        )
+
+    loads = [
+        pltpu.make_async_copy(col_hbm, col_ref, load_sem.at[0]),
+        pltpu.make_async_copy(blocks_hbm, blocks_ref, load_sem.at[1]),
+        pltpu.make_async_copy(coupling_hbm, coupling_ref, load_sem.at[2]),
+        pltpu.make_async_copy(row_hbm, row_ref, load_sem.at[3]),
+    ]
+    for load in loads:
+        load.start()
+
+    b_recv[...] = jnp.zeros_like(b_recv)
+    e_recv[...] = jnp.zeros_like(e_recv)
+    c_recv[...] = jnp.zeros_like(c_recv)
+    d_recv[...] = jnp.zeros_like(d_recv)
+
+    barrier = pltpu.get_barrier_semaphore()
+    for dt in range(T):
+        for dr in range(RK):
+            if dt or dr:
+                pl.semaphore_signal(
+                    barrier,
+                    inc=1,
+                    device_id=(lax.rem(t + dt, T), lax.rem(r + dr, RK)),
+                    device_id_type=pl.DeviceIdType.MESH,
+                )
+
+    pieces = jnp.concatenate(
+        split_bf16(direction_ref[...], 3) + split_bf16(residual_ref[...], 3), axis=0
+    )
+    for q in range(rows):
+        perm = perm_ref[q : q + 1, :]
+        low = lax.bitwise_and(perm, 127)
+        high = lax.shift_right_logical(perm, 7)
+        onehot = (iota((128, 128), 0) == low).astype(f32).astype(bf16)
+        onehot_ref[q] = onehot
+        looked = dot_nn(pieces, onehot)
+        mask = iota((rows, 128), 0) == high
+        d_rows = (looked[0:rows] + looked[rows : 2 * rows]) + looked[2 * rows : 3 * rows]
+        r_rows = (looked[3 * rows : 4 * rows] + looked[4 * rows : 5 * rows]) + looked[5 * rows :]
+        c, k = q // pr, q % pr
+        a_send[c, k : k + 1, :] = jnp.sum(jnp.where(mask, d_rows, 0.0), axis=0, keepdims=True)
+        a_send[c, pr + k : pr + k + 1, :] = jnp.sum(
+            jnp.where(mask, r_rows, 0.0), axis=0, keepdims=True
+        )
+
+    pl.semaphore_wait(barrier, T * RK - 1)
+
+    a_recv[t] = a_send[t]
+    for off in range(1, T):
+        c = lax.rem(t + off, T)
+        remote(a_send.at[c], a_recv.at[t], a_ss.at[c], a_rs.at[t], c, r).start()
+
+    slots_ref[...] = jnp.zeros_like(slots_ref)
+    slots_ref[0:1, 0:NBS] = target_ref[...]
+    slots_ref[1:2, 0:NBS] = leaf_ref[...]
+    diagonal = iota((NBP, 128), 0) == iota((NBP, 128), 1)
+    target_row = slots_ref[0:1, :]
+    leaf_row = slots_ref[1:2, :]
+    target_col = jnp.sum(jnp.where(diagonal, target_row, 0), axis=1, keepdims=True)
+    leaf_col = jnp.sum(jnp.where(diagonal, leaf_row, 0), axis=1, keepdims=True)
+    live = iota((1, 128), 1) < live_ref[...]
+    spread_hot = (
+        ((iota((3 * gt, 128), 0) == lax.shift_right_logical(target_row, 1)) & live)
+        .astype(f32)
+        .astype(bf16)[:, :NBP]
+    )
+    pick_hot = (iota((NBP, 3 * gt), 1) == lax.shift_right_logical(target_col, 1)).astype(f32).astype(bf16)
+    leaf_hot = (iota((NBP, rows), 1) == leaf_col).astype(f32).astype(bf16)
+    leaf_spread = ((iota((rows, 128), 0) == leaf_row) & live).astype(f32).astype(bf16)[:, :NBP]
+    odd = lax.bitwise_and(target_col, 1) == 1
+    upper = iota((NBP, 128), 1) >= LD
+    for k in range(KC):
+        for g in range(G):
+            weight_s[k * G + g : k * G + g + 1, :] = weight_ref[k : k + 1, g * 128 : (g + 1) * 128]
+    values_s[...] = jnp.zeros_like(values_s)
+    loads[0].wait()
+    loads[1].wait()
+
+    for off in range(1, T):
+        s = lax.rem(t + off, T)
+        remote(a_send.at[s], a_recv.at[s], a_ss.at[s], a_rs.at[s], s, r).wait_recv()
+    for s in range(T):
+        vec_f[s * pr : (s + 1) * pr, :] = a_recv[s, 0:pr, :]
+        res_f[s * pr : (s + 1) * pr, :] = a_recv[s, pr : 2 * pr, :]
+
+    vec_row = jnp.concatenate([vec_f[q : q + 1, :] for q in range(rows)], axis=1).astype(bf16)
+    b_send[:, 0:WR] = dot_nt(vec_row, col_ref[...])
+
+    def far(c):
+        return jnp.abs(c - t) > 1
+
+    for off in range(1, T):
+        c = lax.rem(t + off, T)
+
+        @pl.when(far(c))
+        def _():
+            for k in range(RK):
+                remote(
+                    b_send, b_recv.at[me], b_ss.at[c * RK + k], b_rs.at[me], c, k
+                ).start()
+
+    picked = dot_nn(leaf_hot, vec_f[...].astype(bf16)).astype(bf16)
+    for b in range(NBS):
+        values_s[b : b + 1, :] = dot_nt(
+            picked[b : b + 1, :], blocks_ref[b * KI : (b + 1) * KI, :]
+        )
+    for k in range(KC):
+        part = values_s[:, (k // 2) * 128 : (k // 2 + 1) * 128]
+        rolled = pltpu.roll(part, LD, 1)
+        moved = jnp.where(odd, rolled, part) if k % 2 == 0 else jnp.where(odd, part, rolled)
+        moved = jnp.where(upper == odd, moved, 0.0)
+        head, tail = split_bf16(moved, 2)
+        summed = dot_nn(spread_hot, head) + dot_nn(spread_hot, tail)
+        for o in range(3):
+            for k2 in range(RK):
+                start = o * gt + k2 * G
+                c_send[o, k2, k * G : (k + 1) * G, :] = summed[start : start + G, :]
+    for o in range(3):
+        for k2 in range(RK):
+            c_out = c_send[o, k2].astype(bf16)
+            c_bf = c_out
+            d_send[1 + o * RK + k2] = c_bf
+
+    def inside(c):
+        return (c >= 0) & (c < T)
+
+    def near_copies(source, landing, ss, rs, mirrored, act):
+        for o in (0, 2, 1):
+            there = t + (1 - o if mirrored else o - 1)
+
+            @pl.when(inside(there))
+            def _():
+                for dr in range(RK):
+                    if o == 1 and dr == 0:
+                        continue
+                    k2 = lax.rem(r + dr, RK)
+                    act(
+                        remote(
+                            source(o, k2), landing.at[o, r], ss.at[o, k2], rs.at[o, r], there, k2
+                        )
+                    )
+
+    def near_waits(landing, ss, rs, mirrored):
+        for o in (1, 0, 2):
+            there = t + (o - 1 if mirrored else 1 - o)
+
+            @pl.when(inside(there))
+            def _():
+                for dr in range(RK):
+                    if o == 1 and dr == 0:
+                        continue
+                    k2 = lax.rem(r + dr, RK)
+                    remote(
+                        landing.at[o, k2], landing.at[o, k2], ss.at[o, k2], rs.at[o, k2], t, k2
+                    ).wait_recv()
+
+    def c_source(o, k2):
+        return d_send.at[1 + o * RK + k2]
+
+    def d_source(o, k2):
+        return d_send.at[0]
+
+    near_copies(c_source, c_recv, c_ss, c_rs, False, lambda copy: copy.start())
+
+    loads[2].wait()
+    loads[3].wait()
+    for off in range(1, T):
+        c = lax.rem(t + off, T)
+
+        @pl.when(far(c))
+        def _():
+            for k in range(RK):
+                slot = c * RK + k
+                remote(b_send, b_recv.at[slot], b_ss.at[slot], b_rs.at[slot], c, k).wait_recv()
+
+    far_coef = jnp.zeros((1, WR), f32)
+    for c in range(T):
+        coef = b_recv[c * RK]
+        for k in range(1, RK):
+            coef = coef + b_recv[c * RK + k]
+        far_coef = far_coef + dot_nt(coef[:, 0:WR].astype(bf16), coupling_ref[c])
+    far_row = dot_nn(far_coef.astype(bf16), row_ref[...])
+    for m in range(KG):
+        far_s[m : m + 1, :] = far_row[:, m * 128 : (m + 1) * 128]
+
+    near_waits(c_recv, c_ss, c_rs, False)
+    own = jnp.zeros((KG, 128), f32)
+    for k2 in range(RK):
+        own = own + jnp.where(r == k2, c_send[1, k2], 0.0)
+    near = own
+    for o in range(3):
+        for k2 in range(RK):
+            near = near + c_recv[o, k2].astype(f32)
+    weighted = (weight_s[...] * (far_s[...] + near)).astype(bf16)
+    d_send[0] = weighted
+    weighted_f[...] = weighted.astype(f32)
+    near_copies(d_source, d_recv, d_ss, d_rs, True, lambda copy: copy.start())
+    d_recv[1, r] = weighted
+
+    weighted_row = jnp.concatenate([weighted_f[m : m + 1, :] for m in range(KG)], axis=1)
+    back_part = dot_nt(weighted_row.astype(bf16), row_ref[...])
+    back_two = jnp.concatenate(split_bf16(back_part, 2), axis=0)
+    for c in range(T):
+        two = dot_nn(back_two, coupling_ref[c])
+        e_send[c, :, 0:WR] = two[0:1, :] + two[1:2, :]
+    for off in range(1, T):
+        c = lax.rem(t + off, T)
+
+        @pl.when(far(c))
+        def _():
+            for k in range(RK):
+                remote(
+                    e_send.at[c], e_recv.at[me], e_ss.at[c * RK + k], e_rs.at[me], c, k
+                ).start()
+
+    near_waits(d_recv, d_ss, d_rs, True)
+    chosen = []
+    for k in range(KC):
+        window = jnp.concatenate(
+            [
+                d_recv[o, k2, :, :].astype(f32)[k * G : (k + 1) * G, :]
+                for o in range(3)
+                for k2 in range(RK)
+            ],
+            axis=0,
+        ).astype(bf16)
+        found = dot_nn(pick_hot, window)
+        rolled = pltpu.roll(found, LD, 1)
+        chosen.append(
+            jnp.where(odd, rolled, found) if k % 2 == 0 else jnp.where(odd, found, rolled)
+        )
+    chosen_rows = jnp.concatenate(
+        [jnp.where(upper, chosen[2 * m + 1], chosen[2 * m]) for m in range(KC // 2)], axis=1
+    ).astype(bf16)
+    for b in range(NBS):
+        values_s[b : b + 1, 0:128] = dot_nn(
+            chosen_rows[b : b + 1, :], blocks_ref[b * KI : (b + 1) * KI, :]
+        )
+    head, tail = split_bf16(values_s[:, 0:128], 2)
+    near_back = dot_nn(leaf_spread, head) + dot_nn(leaf_spread, tail)
+
+    for off in range(1, T):
+        c = lax.rem(t + off, T)
+
+        @pl.when(far(c))
+        def _():
+            for k in range(RK):
+                slot = c * RK + k
+                remote(e_send.at[c], e_recv.at[slot], e_ss.at[slot], e_rs.at[slot], c, k).wait_recv()
+
+    cluster_back = jnp.zeros((1, 128), f32)
+    for slot in range(T * RK):
+        cluster_back = cluster_back + e_recv[slot]
+    far_back = dot_nn(cluster_back[:, 0:WR].astype(bf16), col_ref[...])
+    for q in range(rows):
+        far_back_s[q : q + 1, :] = far_back[:, q * 128 : (q + 1) * 128]
+    image = far_back_s[...] + near_back
+    for s in range(T):
+        image_s[s] = image[s * pr : (s + 1) * pr, :]
+    for off in range(1, T):
+        s = lax.rem(t + off, T)
+        remote(image_s.at[s], f_recv.at[t], f_ss.at[s], f_rs.at[t], s, r).start()
+    f_recv[t] = image_s[t]
+
+    vec = vec_f[...]
+    res = res_f[...]
+    normal = image + damping_weight * vec
+
+    def total(x):
+        return jnp.sum(jnp.sum(x, axis=0, keepdims=True), axis=1, keepdims=True)
+
+    lane = iota((1, 128), 1)
+    sums = jnp.where(lane == 0, total(vec * normal), 0.0)
+    sums = jnp.where(lane == 1, total(res * normal), sums)
+    sums = jnp.where(lane == 2, total(normal * normal), sums)
+    sums = jnp.where(lane == 3, total(res * res), sums)
+    g_send[...] = sums
+    g_recv[me] = sums
+    others = [(dt, dr) for dt in range(T) for dr in range(RK) if dt or dr]
+    for dt, dr in others:
+        c, k = lax.rem(t + dt, T), lax.rem(r + dr, RK)
+        remote(g_send, g_recv.at[me], g_ss.at[c * RK + k], g_rs.at[me], c, k).start()
+
+    for off in range(1, T):
+        s = lax.rem(t + off, T)
+        remote(image_s.at[s], f_recv.at[s], f_ss.at[s], f_rs.at[s], s, r).wait_recv()
+    back = jnp.zeros((3 * rows, 128), f32)
+    for q in range(rows):
+        perm = perm_ref[q : q + 1, :]
+        high = lax.shift_right_logical(perm, 7)
+        mask = iota((rows, 128), 0) == high
+        entry = f_recv[q // pr, q % pr : q % pr + 1, :]
+        parts = split_bf16(jnp.where(mask, entry, 0.0), 3)
+        back = back + dot_nt(jnp.concatenate(parts, axis=0), onehot_ref[q])
+    slab = (back[0:rows] + back[rows : 2 * rows]) + back[2 * rows :]
+    image_out[...] = slab + damping_weight * direction_ref[...]
+
+    for dt, dr in others:
+        c, k = lax.rem(t + dt, T), lax.rem(r + dr, RK)
+        slot = c * RK + k
+        remote(g_send, g_recv.at[slot], g_ss.at[slot], g_rs.at[slot], c, k).wait_recv()
+    sums = g_recv[0]
+    for slot in range(1, T * RK):
+        sums = sums + g_recv[slot]
+
+    def pick(i):
+        return jnp.sum(jnp.where(lane == i, sums, 0.0), axis=1, keepdims=True)
+
+    norm_now = pick(3) + tiny_value
+    alpha = norm_now / (pick(0) + tiny_value)
+    norm_next = pick(3) - 2.0 * alpha * pick(1) + alpha * alpha * pick(2)
+    beta = jnp.maximum(norm_next, 0.0) / norm_now
+    alpha_out[...] = jnp.broadcast_to(alpha, alpha_out.shape)
+    beta_out[...] = jnp.broadcast_to(beta, beta_out.shape)
+
+    for off in range(1, T):
+        c = lax.rem(t + off, T)
+        remote(a_send.at[c], a_recv.at[t], a_ss.at[c], a_rs.at[t], c, r).wait_send()
+        remote(image_s.at[c], f_recv.at[t], f_ss.at[c], f_rs.at[t], c, r).wait_send()
+
+        @pl.when(far(c))
+        def _():
+            for k in range(RK):
+                remote(b_send, b_recv.at[me], b_ss.at[c * RK + k], b_rs.at[me], c, k).wait_send()
+                remote(
+                    e_send.at[c], e_recv.at[me], e_ss.at[c * RK + k], e_rs.at[me], c, k
+                ).wait_send()
+
+    near_copies(c_source, c_recv, c_ss, c_rs, False, lambda copy: copy.wait_send())
+    near_copies(d_source, d_recv, d_ss, d_rs, True, lambda copy: copy.wait_send())
+    for dt, dr in others:
+        c, k = lax.rem(t + dt, T), lax.rem(r + dr, RK)
+        remote(g_send, g_recv.at[me], g_ss.at[c * RK + k], g_rs.at[me], c, k).wait_send()
+
+
+def fused(
+    step_now,
+    residual,
+    direction,
+    slab_perm,
+    col_basis,
+    row_basis,
+    coupling,
+    near_blocks,
+    near_leaf,
+    near_target,
+    near_live,
+    data_weight,
+):
+    T, RK = lax.axis_size("tile"), lax.axis_size("rank")
+    N = T * RK
+    rows = direction.shape[0] // 128
+    pr = rows // T
+    NBS, KC = near_blocks.shape[0], near_blocks.shape[1]
+    WR = col_basis.shape[0]
+    G = data_weight.shape[1] // 128
+    KG = KC * G
+    NBP = -(-NBS // 16) * 16
+    f32, bf16 = jnp.float32, jnp.bfloat16
+    res2 = residual.reshape(rows, 128)
+    dir2 = direction.reshape(rows, 128)
+    vmem = pl.BlockSpec(memory_space=pltpu.VMEM)
+    hbm = pl.BlockSpec(memory_space=pl.ANY)
+    row2 = row_basis.reshape(WR, -1)
+    blocks2 = near_blocks.reshape(-1, LEAF)
+    sem = pltpu.SemaphoreType.DMA
+    out = jax.ShapeDtypeStruct((rows, 128), f32)
+    image, alpha, beta = pl.pallas_call(
+        functools.partial(cg_kernel, (T, RK, NBS, KC, WR)),
+        out_shape=(out, out, out),
+        in_specs=[vmem, vmem, vmem, hbm, hbm, hbm, hbm, vmem, vmem, vmem, vmem],
+        out_specs=(vmem, vmem, vmem),
+        scratch_shapes=[
+            pltpu.VMEM(col_basis.shape, bf16),
+            pltpu.VMEM(row2.shape, bf16),
+            pltpu.VMEM(coupling.shape[1:], bf16),
+            pltpu.VMEM(blocks2.shape, bf16),
+            pltpu.VMEM((rows, 128, 128), bf16),
+            pltpu.VMEM((8, 128), jnp.int32),
+            pltpu.VMEM((KG, 128), f32),
+            pltpu.VMEM((KG, 128), f32),
+            pltpu.VMEM((KG, 128), f32),
+            pltpu.VMEM((T, 2 * pr, 128), f32),
+            pltpu.VMEM((T, 2 * pr, 128), f32),
+            pltpu.VMEM((rows, 128), f32),
+            pltpu.VMEM((rows, 128), f32),
+            pltpu.VMEM((1, 128), f32),
+            pltpu.VMEM((N, 1, 128), f32),
+            pltpu.VMEM((3, RK, KG, 128), f32),
+            pltpu.VMEM((3, RK, KG, 128), bf16),
+            pltpu.VMEM((1 + 3 * RK, KG, 128), bf16),
+            pltpu.VMEM((3, RK, KG, 128), bf16),
+            pltpu.VMEM((T, 1, 128), f32),
+            pltpu.VMEM((N, 1, 128), f32),
+            pltpu.VMEM((rows, 128), f32),
+            pltpu.VMEM((T, pr, 128), f32),
+            pltpu.VMEM((T, pr, 128), f32),
+            pltpu.VMEM((1, 128), f32),
+            pltpu.VMEM((N, 1, 128), f32),
+            pltpu.VMEM((NBP, KC * LD), f32),
+            sem((4,)),
+            sem((T,)),
+            sem((T,)),
+            sem((N,)),
+            sem((N,)),
+            sem((3, RK)),
+            sem((3, RK)),
+            sem((3, RK)),
+            sem((3, RK)),
+            sem((N,)),
+            sem((N,)),
+            sem((T,)),
+            sem((T,)),
+            sem((N,)),
+            sem((N,)),
+        ],
+        compiler_params=pltpu.CompilerParams(
+            collective_id=0, has_side_effects=True, vmem_limit_bytes=32 * 1024 * 1024
+        ),
+    )(
+        res2,
+        dir2,
+        slab_perm.reshape(rows, 128),
+        col_basis,
+        row2,
+        coupling[0],
+        blocks2,
+        near_leaf.reshape(1, NBS),
+        near_target.reshape(1, NBS),
+        near_live.reshape(1, 1),
+        data_weight,
+    )
+    new_step = step_now.reshape(rows, 128) + alpha * dir2
+    new_residual = res2 - alpha * image
+    new_direction = new_residual + beta * dir2
+    return tuple(x.reshape(-1) for x in (new_step, new_residual, new_direction))
+
+
 def solution(mesh):
+    def body(*args):
+        piece = args[2].shape[0] // mesh.shape["tile"]
+        return (per_device if piece % 128 else fused)(*args)
+
     return jax.shard_map(
-        per_device,
+        body,
         mesh=mesh,
         in_specs=(
             P(("tile", "rank")),

time: 244 us -> 40.5 us (0.17)
  blocking collectives: 159 us -> 0 us
  Pallas kernels: 0 us -> 29.3 us
  starting transfers between devices: 20.1 us -> 0 us
  local copies, waits for them, and re-layouts: 26.9 us -> 8.74 us
  between operations: 17 us -> 1.31 us
  other arithmetic: 8.11 us -> 0.61 us
  matrix products: 6.13 us -> 0 us
  waiting for transfers between devices: 5.65 us -> 0 us
    psum x3 -> x0, blocking collectives: 85.8 us -> none  [the longest x1 40.5 us: per_device(): norm_next = lax.psum(jnp.sum(new_residual * new_residual), ('tile', 'rank'))]
    unnamed x2 -> x0, blocking collectives: 59.2 us -> none
    pallas_call x0 -> x1, Pallas kernels: none -> 29.3 us  [fused(): pl.pallas_call(functools.partial(cg_kernel, (T, RK, NBS, KC, WR)), out_sh...]
    gather x3 -> x0, local copies, waits for them, and re-layouts: 14.3 us -> none  [the longest x1 13.1 us: per_device(): outgoing = dir_bf[slab_perm].reshape(tile_count, piece_len)]
    ppermute x4 -> x0, starting transfers between devices: 12.8 us -> none  [the longest x2 10.3 us: with_halo(): lax.ppermute(lax.slice_in_dim(block, block.shape[dim] - width, None, axis...]
    all_to_all x1 -> x0, blocking collectives: 8.88 us -> none  [per_device(): lax.all_to_all(cluster_image.reshape(tile_count, piece_len), 'tile', spli...]
    scatter x1 -> x0, local copies, waits for them, and re-layouts: 8.05 us -> none  [per_device(): slab_image = jnp.zeros((slab_len,), jnp.float32).at[slab_perm].set(returned)]
    all_to_all x1 -> x0, starting transfers between devices: 7.28 us -> none  [per_device(): lax.all_to_all(outgoing, 'tile', split_axis=0, concat_axis=0, tiled=True)]
  transfers between devices with their start and end apart: 6 -> 0, of which waited for: 1 -> 0; matrix products, arithmetic and copies ran while one was open for 2% -> 0% of each run, Pallas kernels for 0% -> 0%
where the time goes in v1:
time: 40.5 us; the launch traced here: 40 us
  Pallas kernels  29.3 us (72%)
  local copies, waits for them, and re-layouts  8.74 us (22%)
  between operations  1.31 us (3%)
  other arithmetic  0.61 us (2%)
    pallas_call x1, Pallas kernels, fused(): pl.pallas_call(functools.partial(cg_kernel, (T, RK, NBS, KC, WR)), out_sh...  29.3 us
    unnamed x20, local copies, waits for them, and re-layouts  7.55 us
    reshape x1, local copies, waits for them, and re-layouts, fused(): row2 = row_basis.reshape(WR, -1)  1.19 us

profile of v1, /device:TPU:0, one launch (start us, length us, event | category | flops | bytes accessed | tf_op | source)
XLA Modules:
  0.0 40.0 jit_solution(11516207965811237586)
XLA Ops:
  1.3 1.2 %copy.17 = bf16[6,8,8,1024]{3,2,0,1:T(8,128)(2,1)S(1)} copy(bf16[6,8,8,1024]{3,2,1,0:T(8,128)(2,1)} %bitcast.36) | data formatting | bytes 1572864 | tf_op jit(solution)/shard_map/reshape | solution.py:592
  2.5 0.0 copy-start
  2.5 1.5 %copy-done = bf16[20,6,64,128]{3,2,1,0:T(8,128)(2,1)S(1)} copy-done((bf16[20,6,64,128]{3,2,1,0:T(8,128)(2,1)S(1)}, bf16[20,6,64,128]{3,2,1,0:T(8,128)(2,1)}, u32[]{:S(2)}) %copy-start) | copy-done | bytes 1966104
  4.0 0.0 copy-start.1
  4.0 0.9 %copy-done.1 = bf16[64,2048]{1,0:T(8,128)(2,1)S(1)} copy-done((bf16[64,2048]{1,0:T(8,128)(2,1)S(1)}, bf16[64,2048]{1,0:T(8,128)(2,1)}, u32[]{:S(2)}) %copy-start.1) | copy-done | bytes 262168
  5.0 0.0 copy-start.2
  5.0 0.9 %copy-done.2 = bf16[1,8,64,64]{3,2,1,0:T(8,128)(2,1)S(1)} copy-done((bf16[1,8,64,64]{3,2,1,0:T(8,128)(2,1)S(1)}, bf16[1,8,64,64]{3,2,1,0:T(8,128)(2,1)}, u32[]{:S(2)}) %copy-start.2) | copy-done | bytes 65560
  5.9 0.0 copy-start.3
  5.9 0.8 %copy-done.3 = f32[6,1024]{1,0:T(8,128)S(1)} copy-done((f32[6,1024]{1,0:T(8,128)S(1)}, f32[6,1024]{1,0:T(8,128)}, u32[]{:S(2)}) %copy-start.3) | copy-done | bytes 24600
  6.6 0.0 copy-start.4
  6.6 0.7 %copy-done.4 = f32[2048]{0:T(1024)S(1)} copy-done((f32[2048]{0:T(1024)S(1)}, f32[2048]{0:T(1024)}, u32[]{:S(2)}) %copy-start.4) | copy-done | bytes 8216
  7.3 0.0 copy-start.5
  7.3 0.7 %copy-done.5 = f32[2048]{0:T(1024)S(1)} copy-done((f32[2048]{0:T(1024)S(1)}, f32[2048]{0:T(1024)}, u32[]{:S(2)}) %copy-start.5) | copy-done | bytes 8216
  8.0 0.0 copy-start.6
  8.0 0.7 %copy-done.6 = s32[2048]{0:T(1024)S(1)} copy-done((s32[2048]{0:T(1024)S(1)}, s32[2048]{0:T(1024)}, u32[]{:S(2)}) %copy-start.6) | copy-done | bytes 8216
  8.7 0.0 copy-start.7
  8.7 0.7 %copy-done.7 = s32[20]{0:T(128)S(1)} copy-done((s32[20]{0:T(128)S(1)}, s32[20]{0:T(128)}, u32[]{:S(2)}) %copy-start.7) | copy-done | bytes 104
  9.4 0.0 copy-start.8
  9.4 0.7 %copy-done.8 = s32[20]{0:T(128)S(1)} copy-done((s32[20]{0:T(128)S(1)}, s32[20]{0:T(128)}, u32[]{:S(2)}) %copy-start.8) | copy-done | bytes 104
  10.0 0.0 copy-start.9
  10.0 29.3 %shard_map.139 = (f32[16,128]{1,0:T(8,128)S(1)}, f32[16,128]{1,0:T(8,128)S(1)}, f32[16,128]{1,0:T(8,128)S(1)}) custom-call(f32[16,128]{1,0:T(8,128)S(1)} %bitcast.31, f32[16,128]{1,0:T(8,128)S(1)} %bitcast.32, s32[16,128]{1,0:T(8,128)S(1)} %bitcast.33, bf16[64,2048]{1,0:T(8,128)(2,1)S(1)} %copy-done.1, bf16[64,6144]{1,0:T(8,128)(2,1)S(1)} %bitcast.28, ...), custom_call_target="tpu_custom_call" | custom-call | tf_op jit(solution)/shard_map/pallas_call | solution.py:596
  39.4 0.0 copy-done.9
  39.4 0.6 %add_bitcast_fusion = (f32[2048]{0:T(1024)}, f32[2048]{0:T(1024)}, f32[2048]{0:T(1024)}) fusion(f32[16,128]{1,0:T(8,128)S(1)} %get-tuple-element.8, f32[2048]{0:T(1024)S(1)} %copy-done.5, f32[16,128]{1,0:T(8,128)S(1)} %get-tuple-element.6, f32[16,128]{1,0:T(8,128)S(1)} %get-tuple-element.7, f32[2048]{0:T(1024)S(1)} %copy-done.4, f32[2048]{0:T(1024)S(1)} %copy-done.9), kind=kLoop, calls=%fused_computation.2 | loop fusion | flops 12288 | bytes 73728 | tf_op jit(solution)/shard_map/reshape | solution.py:664
Async XLA Ops:
  2.5 1.5 %copy-start = (bf16[20,6,64,128]{3,2,1,0:T(8,128)(2,1)S(1)}, bf16[20,6,64,128]{3,2,1,0:T(8,128)(2,1)}, u32[]{:S(2)}) copy-start(bf16[20,6,64,128]{3,2,1,0:T(8,128)(2,1)} %param.19) | copy-start | bytes 5898244
  4.0 0.9 %copy-start.1 = (bf16[64,2048]{1,0:T(8,128)(2,1)S(1)}, bf16[64,2048]{1,0:T(8,128)(2,1)}, u32[]{:S(2)}) copy-start(bf16[64,2048]{1,0:T(8,128)(2,1)} %col_hbm.1) | copy-start | bytes 786436
  5.0 0.9 %copy-start.2 = (bf16[1,8,64,64]{3,2,1,0:T(8,128)(2,1)S(1)}, bf16[1,8,64,64]{3,2,1,0:T(8,128)(2,1)}, u32[]{:S(2)}) copy-start(bf16[1,8,64,64]{3,2,1,0:T(8,128)(2,1)} %param.18) | copy-start | bytes 196612
  5.9 0.8 %copy-start.3 = (f32[6,1024]{1,0:T(8,128)S(1)}, f32[6,1024]{1,0:T(8,128)}, u32[]{:S(2)}) copy-start(f32[6,1024]{1,0:T(8,128)} %weight_ref.1) | copy-start | bytes 73732
  6.6 0.7 %copy-start.4 = (f32[2048]{0:T(1024)S(1)}, f32[2048]{0:T(1024)}, u32[]{:S(2)}) copy-start(f32[2048]{0:T(1024)} %param.13) | copy-start | bytes 24580
  7.3 0.7 %copy-start.5 = (f32[2048]{0:T(1024)S(1)}, f32[2048]{0:T(1024)}, u32[]{:S(2)}) copy-start(f32[2048]{0:T(1024)} %param.14) | copy-start | bytes 24580
  8.0 0.7 %copy-start.6 = (s32[2048]{0:T(1024)S(1)}, s32[2048]{0:T(1024)}, u32[]{:S(2)}) copy-start(s32[2048]{0:T(1024)} %param.15) | copy-start | bytes 24580
  8.7 0.7 %copy-start.7 = (s32[20]{0:T(128)S(1)}, s32[20]{0:T(128)}, u32[]{:S(2)}) copy-start(s32[20]{0:T(128)} %param.20) | copy-start | bytes 244
  9.4 0.7 %copy-start.8 = (s32[20]{0:T(128)S(1)}, s32[20]{0:T(128)}, u32[]{:S(2)}) copy-start(s32[20]{0:T(128)} %param.21) | copy-start | bytes 244
  10.0 29.4 %copy-start.9 = (f32[2048]{0:T(1024)S(1)}, f32[2048]{0:T(1024)}, u32[]{:S(2)}) copy-start(f32[2048]{0:T(1024)} %param.12) | copy-start | bytes 24580

commit v2 on v1

--- a/solution.py
+++ b/solution.py
@@ -147,20 +147,26 @@
 
 def cg_kernel(
     dims,
-    residual_ref,
-    direction_ref,
-    perm_ref,
+    residual_hbm,
+    direction_hbm,
+    perm_hbm,
     col_hbm,
     row_hbm,
     coupling_hbm,
     blocks_hbm,
-    leaf_ref,
-    target_ref,
-    live_ref,
-    weight_ref,
+    leaf_hbm,
+    target_hbm,
+    live_smem,
+    weight_hbm,
     image_out,
     alpha_out,
     beta_out,
+    residual_ref,
+    direction_ref,
+    perm_ref,
+    leaf_ref,
+    target_ref,
+    weight_ref,
     col_ref,
     row_ref,
     coupling_ref,
@@ -206,9 +212,9 @@
 ):
     T, RK, NBS, KC, WR = dims
     bf16, f32 = jnp.bfloat16, jnp.float32
-    rows = direction_ref.shape[0]
+    rows = direction_hbm.shape[0]
     pr = rows // T
-    G = weight_ref.shape[1] // 128
+    G = weight_hbm.shape[1] // 128
     KG = KC * G
     gt = G * RK
     NBP = values_s.shape[0]
@@ -227,11 +233,21 @@
             device_id_type=pl.DeviceIdType.MESH,
         )
 
+    operands = [
+        (direction_hbm, direction_ref),
+        (perm_hbm, perm_ref),
+        (residual_hbm, residual_ref),
+        (leaf_hbm, leaf_ref),
+        (target_hbm, target_ref),
+        (weight_hbm, weight_ref),
+        (col_hbm, col_ref),
+        (blocks_hbm, blocks_ref),
+        (coupling_hbm, coupling_ref),
+        (row_hbm, row_ref),
+    ]
     loads = [
-        pltpu.make_async_copy(col_hbm, col_ref, load_sem.at[0]),
-        pltpu.make_async_copy(blocks_hbm, blocks_ref, load_sem.at[1]),
-        pltpu.make_async_copy(coupling_hbm, coupling_ref, load_sem.at[2]),
-        pltpu.make_async_copy(row_hbm, row_ref, load_sem.at[3]),
+        pltpu.make_async_copy(source, held, load_sem.at[i])
+        for i, (source, held) in enumerate(operands)
     ]
     for load in loads:
         load.start()
@@ -252,6 +268,8 @@
                     device_id_type=pl.DeviceIdType.MESH,
                 )
 
+    for load in loads[:3]:
+        load.wait()
     pieces = jnp.concatenate(
         split_bf16(direction_ref[...], 3) + split_bf16(residual_ref[...], 3), axis=0
     )
@@ -278,6 +296,8 @@
         c = lax.rem(t + off, T)
         remote(a_send.at[c], a_recv.at[t], a_ss.at[c], a_rs.at[t], c, r).start()
 
+    for load in loads[3:8]:
+        load.wait()
     slots_ref[...] = jnp.zeros_like(slots_ref)
     slots_ref[0:1, 0:NBS] = target_ref[...]
     slots_ref[1:2, 0:NBS] = leaf_ref[...]
@@ -286,7 +306,7 @@
     leaf_row = slots_ref[1:2, :]
     target_col = jnp.sum(jnp.where(diagonal, target_row, 0), axis=1, keepdims=True)
     leaf_col = jnp.sum(jnp.where(diagonal, leaf_row, 0), axis=1, keepdims=True)
-    live = iota((1, 128), 1) < live_ref[...]
+    live = iota((1, 128), 1) < live_smem[0]
     spread_hot = (
         ((iota((3 * gt, 128), 0) == lax.shift_right_logical(target_row, 1)) & live)
         .astype(f32)
@@ -301,8 +321,6 @@
         for g in range(G):
             weight_s[k * G + g : k * G + g + 1, :] = weight_ref[k : k + 1, g * 128 : (g + 1) * 128]
     values_s[...] = jnp.zeros_like(values_s)
-    loads[0].wait()
-    loads[1].wait()
 
     for off in range(1, T):
         s = lax.rem(t + off, T)
@@ -390,8 +408,8 @@
 
     near_copies(c_source, c_recv, c_ss, c_rs, False, lambda copy: copy.start())
 
-    loads[2].wait()
-    loads[3].wait()
+    loads[8].wait()
+    loads[9].wait()
     for off in range(1, T):
         c = lax.rem(t + off, T)
 
@@ -407,9 +425,11 @@
         for k in range(1, RK):
             coef = coef + b_recv[c * RK + k]
         far_coef = far_coef + dot_nt(coef[:, 0:WR].astype(bf16), coupling_ref[c])
-    far_row = dot_nn(far_coef.astype(bf16), row_ref[...])
-    for m in range(KG):
-        far_s[m : m + 1, :] = far_row[:, m * 128 : (m + 1) * 128]
+    far_bf = far_coef.astype(bf16)
+    for k in range(KC):
+        far_row = dot_nn(far_bf, row_ref[k])
+        for g in range(G):
+            far_s[k * G + g : k * G + g + 1, :] = far_row[:, g * 128 : (g + 1) * 128]
 
     near_waits(c_recv, c_ss, c_rs, False)
     own = jnp.zeros((KG, 128), f32)
@@ -425,8 +445,12 @@
     near_copies(d_source, d_recv, d_ss, d_rs, True, lambda copy: copy.start())
     d_recv[1, r] = weighted
 
-    weighted_row = jnp.concatenate([weighted_f[m : m + 1, :] for m in range(KG)], axis=1)
-    back_part = dot_nt(weighted_row.astype(bf16), row_ref[...])
+    back_part = jnp.zeros((1, WR), f32)
+    for k in range(KC):
+        weighted_row = jnp.concatenate(
+            [weighted_f[k * G + g : k * G + g + 1, :] for g in range(G)], axis=1
+        )
+        back_part = back_part + dot_nt(weighted_row.astype(bf16), row_ref[k])
     back_two = jnp.concatenate(split_bf16(back_part, 2), axis=0)
     for c in range(T):
         two = dot_nn(back_two, coupling_ref[c])
@@ -588,19 +612,25 @@
     res2 = residual.reshape(rows, 128)
     dir2 = direction.reshape(rows, 128)
     vmem = pl.BlockSpec(memory_space=pltpu.VMEM)
-    hbm = pl.BlockSpec(memory_space=pl.ANY)
-    row2 = row_basis.reshape(WR, -1)
+    hbm = pl.BlockSpec(memory_space=pltpu.HBM)
+    row3 = row_basis.transpose(1, 0, 2)
     blocks2 = near_blocks.reshape(-1, LEAF)
     sem = pltpu.SemaphoreType.DMA
     out = jax.ShapeDtypeStruct((rows, 128), f32)
     image, alpha, beta = pl.pallas_call(
         functools.partial(cg_kernel, (T, RK, NBS, KC, WR)),
         out_shape=(out, out, out),
-        in_specs=[vmem, vmem, vmem, hbm, hbm, hbm, hbm, vmem, vmem, vmem, vmem],
+        in_specs=[hbm] * 9 + [pl.BlockSpec(memory_space=pltpu.SMEM), hbm],
         out_specs=(vmem, vmem, vmem),
         scratch_shapes=[
+            pltpu.VMEM((rows, 128), f32),
+            pltpu.VMEM((rows, 128), f32),
+            pltpu.VMEM((rows, 128), jnp.int32),
+            pltpu.VMEM((1, NBS), jnp.int32),
+            pltpu.VMEM((1, NBS), jnp.int32),
+            pltpu.VMEM(data_weight.shape, f32),
             pltpu.VMEM(col_basis.shape, bf16),
-            pltpu.VMEM(row2.shape, bf16),
+            pltpu.VMEM(row3.shape, bf16),
             pltpu.VMEM(coupling.shape[1:], bf16),
             pltpu.VMEM(blocks2.shape, bf16),
             pltpu.VMEM((rows, 128, 128), bf16),
@@ -626,7 +656,7 @@
             pltpu.VMEM((1, 128), f32),
             pltpu.VMEM((N, 1, 128), f32),
             pltpu.VMEM((NBP, KC * LD), f32),
-            sem((4,)),
+            sem((10,)),
             sem((T,)),
             sem((T,)),
             sem((N,)),
@@ -643,19 +673,19 @@
             sem((N,)),
         ],
         compiler_params=pltpu.CompilerParams(
-            collective_id=0, has_side_effects=True, vmem_limit_bytes=32 * 1024 * 1024
+            collective_id=0, has_side_effects=True, vmem_limit_bytes=64 * 1024 * 1024
         ),
     )(
         res2,
         dir2,
         slab_perm.reshape(rows, 128),
         col_basis,
-        row2,
+        row3,
         coupling[0],
         blocks2,
         near_leaf.reshape(1, NBS),
         near_target.reshape(1, NBS),
-        near_live.reshape(1, 1),
+        near_live,
         data_weight,
     )
     new_step = step_now.reshape(rows, 128) + alpha * dir2

time: 40.5 us -> 32.4 us (0.80)
  local copies, waits for them, and re-layouts: 8.74 us -> 0 us
  other arithmetic: 0.61 us -> 1.4 us
    unnamed x20 -> x0, local copies, waits for them, and re-layouts: 7.55 us -> none
    reshape x1 -> x0, local copies, waits for them, and re-layouts: 1.19 us -> none  [fused(): row2 = row_basis.reshape(WR, -1)]
    reshape x1, other arithmetic: 0.61 us -> 1.4 us  [fused(): x.reshape(-1)]
where the time goes in v2:
time: 32.4 us; the launch traced here: 32.2 us
  Pallas kernels  29.5 us (91%)
  other arithmetic  1.4 us (4%)
  between operations  1.29 us (4%)
    pallas_call x1, Pallas kernels, fused(): pl.pallas_call(functools.partial(cg_kernel, (T, RK, NBS, KC, WR)), out_sh...  29.5 us
    reshape x1, other arithmetic, fused(): x.reshape(-1)  1.4 us

profile of v2, /device:TPU:0, one launch (start us, length us, event | category | flops | bytes accessed | tf_op | source)
XLA Modules:
  0.0 32.2 jit_solution(2916547362855503245)
XLA Ops:
  1.3 29.5 %shard_map.139 = (f32[16,128]{1,0:T(8,128)}, f32[16,128]{1,0:T(8,128)}, f32[16,128]{1,0:T(8,128)}) custom-call(f32[16,128]{1,0:T(8,128)} %bitcast.28, f32[16,128]{1,0:T(8,128)} %bitcast.29, s32[16,128]{1,0:T(8,128)} %bitcast.30, bf16[64,2048]{1,0:T(8,128)(2,1)} %col_hbm.1, bf16[6,64,1024]{2,1,0:T(8,128)(2,1)} %bitcast.26, bf16[8,64,64]{2,1,0:T(8,128)(2,1)} %bitcast.27, ...), custom_call_target="tpu_custom_call" | custom-call | tf_op jit(solution)/shard_map/pallas_call | solution.py:620
  30.8 1.4 %add_bitcast_fusion = (f32[2048]{0:T(1024)}, f32[2048]{0:T(1024)}, f32[2048]{0:T(1024)}) fusion(f32[16,128]{1,0:T(8,128)} %get-tuple-element.8, f32[2048]{0:T(1024)} %param.14, f32[16,128]{1,0:T(8,128)} %get-tuple-element.6, f32[16,128]{1,0:T(8,128)} %get-tuple-element.7, f32[2048]{0:T(1024)} %param.13, f32[2048]{0:T(1024)} %param.12), kind=kLoop, calls=%fused_computation.2 | loop fusion | flops 12288 | bytes 73728 | tf_op jit(solution)/shard_map/reshape | solution.py:694

commit v3 on v2

--- a/solution.py
+++ b/solution.py
@@ -182,29 +182,36 @@
     res_f,
     b_send,
     b_recv,
+    b_all,
     c_send,
     c_recv,
     d_send,
     d_recv,
     e_send,
     e_recv,
+    e_sum,
+    e_all,
     far_back_s,
     image_s,
     f_recv,
     g_send,
-    g_recv,
+    g_all,
     values_s,
     load_sem,
     a_ss,
     a_rs,
     b_ss,
     b_rs,
+    b2_ss,
+    b2_rs,
     c_ss,
     c_rs,
     d_ss,
     d_rs,
     e_ss,
     e_rs,
+    e2_ss,
+    e2_rs,
     f_ss,
     f_rs,
     g_ss,
@@ -221,7 +228,6 @@
     KI = KC * LD
     t = lax.axis_index("tile")
     r = lax.axis_index("rank")
-    me = t * RK + r
 
     def remote(src, dst, ss, rs, tile, rank):
         return pltpu.make_async_remote_copy(
@@ -232,6 +238,21 @@
             device_id=(tile, rank),
             device_id_type=pl.DeviceIdType.MESH,
         )
+
+    def inside(c):
+        return (c >= 0) & (c < T)
+
+    def far(c):
+        return jnp.abs(c - t) > 1
+
+    def rank_copies(source, landing, ss, rs):
+        peers = [lax.rem(r + dr, RK) for dr in range(1, RK)]
+        return [remote(source, landing.at[r], ss.at[k], rs.at[r], t, k) for k in peers]
+
+    def rank_waits(landing, ss, rs):
+        for dr in range(1, RK):
+            k = lax.rem(r + dr, RK)
+            remote(landing.at[k], landing.at[k], ss.at[k], rs.at[k], t, k).wait_recv()
 
     operands = [
         (direction_hbm, direction_ref),
@@ -258,15 +279,24 @@
     d_recv[...] = jnp.zeros_like(d_recv)
 
     barrier = pltpu.get_barrier_semaphore()
-    for dt in range(T):
-        for dr in range(RK):
-            if dt or dr:
-                pl.semaphore_signal(
-                    barrier,
-                    inc=1,
-                    device_id=(lax.rem(t + dt, T), lax.rem(r + dr, RK)),
-                    device_id_type=pl.DeviceIdType.MESH,
-                )
+
+    def greet(tile, rank):
+        pl.semaphore_signal(
+            barrier, inc=1, device_id=(tile, rank), device_id_type=pl.DeviceIdType.MESH
+        )
+
+    for dt in range(1, T):
+        greet(lax.rem(t + dt, T), r)
+    for dr in range(1, RK):
+        greet(t, lax.rem(r + dr, RK))
+    for side in (-1, 1):
+
+        @pl.when(inside(t + side))
+        def _():
+            for dr in range(1, RK):
+                greet(t + side, lax.rem(r + dr, RK))
+
+    sides = jnp.where(t > 0, 1, 0) + jnp.where(t < T - 1, 1, 0)
 
     for load in loads[:3]:
         load.wait()
@@ -289,7 +319,7 @@
             jnp.where(mask, r_rows, 0.0), axis=0, keepdims=True
         )
 
-    pl.semaphore_wait(barrier, T * RK - 1)
+    pl.semaphore_wait(barrier, T - 1 + (RK - 1) * (1 + sides))
 
     a_recv[t] = a_send[t]
     for off in range(1, T):
@@ -332,24 +362,28 @@
     vec_row = jnp.concatenate([vec_f[q : q + 1, :] for q in range(rows)], axis=1).astype(bf16)
     b_send[:, 0:WR] = dot_nt(vec_row, col_ref[...])
 
-    def far(c):
-        return jnp.abs(c - t) > 1
-
     for off in range(1, T):
         c = lax.rem(t + off, T)
 
         @pl.when(far(c))
         def _():
-            for k in range(RK):
-                remote(
-                    b_send, b_recv.at[me], b_ss.at[c * RK + k], b_rs.at[me], c, k
-                ).start()
+            remote(b_send, b_recv.at[t], b_ss.at[c], b_rs.at[t], c, r).start()
 
     picked = dot_nn(leaf_hot, vec_f[...].astype(bf16)).astype(bf16)
     for b in range(NBS):
         values_s[b : b + 1, :] = dot_nt(
             picked[b : b + 1, :], blocks_ref[b * KI : (b + 1) * KI, :]
         )
+    for off in range(1, T):
+        c = lax.rem(t + off, T)
+
+        @pl.when(far(c))
+        def _():
+            remote(b_send, b_recv.at[c], b_ss.at[c], b_rs.at[c], c, r).wait_recv()
+
+    for copy in rank_copies(b_recv, b_all, b2_ss, b2_rs):
+        copy.start()
+    b_all[r] = b_recv[...]
     for k in range(KC):
         part = values_s[:, (k // 2) * 128 : (k // 2 + 1) * 128]
         rolled = pltpu.roll(part, LD, 1)
@@ -367,9 +401,6 @@
             c_bf = c_out
             d_send[1 + o * RK + k2] = c_bf
 
-    def inside(c):
-        return (c >= 0) & (c < T)
-
     def near_copies(source, landing, ss, rs, mirrored, act):
         for o in (0, 2, 1):
             there = t + (1 - o if mirrored else o - 1)
@@ -410,20 +441,12 @@
 
     loads[8].wait()
     loads[9].wait()
-    for off in range(1, T):
-        c = lax.rem(t + off, T)
-
-        @pl.when(far(c))
-        def _():
-            for k in range(RK):
-                slot = c * RK + k
-                remote(b_send, b_recv.at[slot], b_ss.at[slot], b_rs.at[slot], c, k).wait_recv()
-
+    rank_waits(b_all, b2_ss, b2_rs)
     far_coef = jnp.zeros((1, WR), f32)
     for c in range(T):
-        coef = b_recv[c * RK]
+        coef = b_all[0, c]
         for k in range(1, RK):
-            coef = coef + b_recv[c * RK + k]
+            coef = coef + b_all[k, c]
         far_coef = far_coef + dot_nt(coef[:, 0:WR].astype(bf16), coupling_ref[c])
     far_bf = far_coef.astype(bf16)
     for k in range(KC):
@@ -460,12 +483,23 @@
 
         @pl.when(far(c))
         def _():
-            for k in range(RK):
-                remote(
-                    e_send.at[c], e_recv.at[me], e_ss.at[c * RK + k], e_rs.at[me], c, k
-                ).start()
+            remote(e_send.at[c], e_recv.at[t], e_ss.at[c], e_rs.at[t], c, r).start()
 
     near_waits(d_recv, d_ss, d_rs, True)
+    for off in range(1, T):
+        c = lax.rem(t + off, T)
+
+        @pl.when(far(c))
+        def _():
+            remote(e_send.at[c], e_recv.at[c], e_ss.at[c], e_rs.at[c], c, r).wait_recv()
+
+    spread_sum = e_recv[0]
+    for c in range(1, T):
+        spread_sum = spread_sum + e_recv[c]
+    e_sum[...] = spread_sum
+    for copy in rank_copies(e_sum, e_all, e2_ss, e2_rs):
+        copy.start()
+    e_all[r] = spread_sum
     chosen = []
     for k in range(KC):
         window = jnp.concatenate(
@@ -491,28 +525,14 @@
     head, tail = split_bf16(values_s[:, 0:128], 2)
     near_back = dot_nn(leaf_spread, head) + dot_nn(leaf_spread, tail)
 
-    for off in range(1, T):
-        c = lax.rem(t + off, T)
-
-        @pl.when(far(c))
-        def _():
-            for k in range(RK):
-                slot = c * RK + k
-                remote(e_send.at[c], e_recv.at[slot], e_ss.at[slot], e_rs.at[slot], c, k).wait_recv()
-
+    rank_waits(e_all, e2_ss, e2_rs)
     cluster_back = jnp.zeros((1, 128), f32)
-    for slot in range(T * RK):
-        cluster_back = cluster_back + e_recv[slot]
+    for k in range(RK):
+        cluster_back = cluster_back + e_all[k]
     far_back = dot_nn(cluster_back[:, 0:WR].astype(bf16), col_ref[...])
     for q in range(rows):
         far_back_s[q : q + 1, :] = far_back[:, q * 128 : (q + 1) * 128]
     image = far_back_s[...] + near_back
-    for s in range(T):
-        image_s[s] = image[s * pr : (s + 1) * pr, :]
-    for off in range(1, T):
-        s = lax.rem(t + off, T)
-        remote(image_s.at[s], f_recv.at[t], f_ss.at[s], f_rs.at[t], s, r).start()
-    f_recv[t] = image_s[t]
 
     vec = vec_f[...]
     res = res_f[...]
@@ -526,16 +546,23 @@
     sums = jnp.where(lane == 1, total(res * normal), sums)
     sums = jnp.where(lane == 2, total(normal * normal), sums)
     sums = jnp.where(lane == 3, total(res * res), sums)
-    g_send[...] = sums
-    g_recv[me] = sums
-    others = [(dt, dr) for dt in range(T) for dr in range(RK) if dt or dr]
-    for dt, dr in others:
-        c, k = lax.rem(t + dt, T), lax.rem(r + dr, RK)
-        remote(g_send, g_recv.at[me], g_ss.at[c * RK + k], g_rs.at[me], c, k).start()
-
+    for s in range(T):
+        image_s[s, 0:pr, :] = image[s * pr : (s + 1) * pr, :]
+        image_s[s, pr : 2 * pr, :] = jnp.broadcast_to(sums, (pr, 128))
+    for off in range(1, T):
+        s = lax.rem(t + off, T)
+        remote(image_s.at[s], f_recv.at[t], f_ss.at[s], f_rs.at[t], s, r).start()
+    f_recv[t] = image_s[t]
     for off in range(1, T):
         s = lax.rem(t + off, T)
         remote(image_s.at[s], f_recv.at[s], f_ss.at[s], f_rs.at[s], s, r).wait_recv()
+    tile_sums = f_recv[0, pr : pr + 1, :]
+    for s in range(1, T):
+        tile_sums = tile_sums + f_recv[s, pr : pr + 1, :]
+    g_send[...] = tile_sums
+    for copy in rank_copies(g_send, g_all, g_ss, g_rs):
+        copy.start()
+    g_all[r] = tile_sums
     back = jnp.zeros((3 * rows, 128), f32)
     for q in range(rows):
         perm = perm_ref[q : q + 1, :]
@@ -547,13 +574,10 @@
     slab = (back[0:rows] + back[rows : 2 * rows]) + back[2 * rows :]
     image_out[...] = slab + damping_weight * direction_ref[...]
 
-    for dt, dr in others:
-        c, k = lax.rem(t + dt, T), lax.rem(r + dr, RK)
-        slot = c * RK + k
-        remote(g_send, g_recv.at[slot], g_ss.at[slot], g_rs.at[slot], c, k).wait_recv()
-    sums = g_recv[0]
-    for slot in range(1, T * RK):
-        sums = sums + g_recv[slot]
+    rank_waits(g_all, g_ss, g_rs)
+    sums = g_all[0]
+    for k in range(1, RK):
+        sums = sums + g_all[k]
 
     def pick(i):
         return jnp.sum(jnp.where(lane == i, sums, 0.0), axis=1, keepdims=True)
@@ -572,17 +596,18 @@
 
         @pl.when(far(c))
         def _():
-            for k in range(RK):
-                remote(b_send, b_recv.at[me], b_ss.at[c * RK + k], b_rs.at[me], c, k).wait_send()
-                remote(
-                    e_send.at[c], e_recv.at[me], e_ss.at[c * RK + k], e_rs.at[me], c, k
-                ).wait_send()
+            remote(b_send, b_recv.at[t], b_ss.at[c], b_rs.at[t], c, r).wait_send()
+            remote(e_send.at[c], e_recv.at[t], e_ss.at[c], e_rs.at[t], c, r).wait_send()
 
     near_copies(c_source, c_recv, c_ss, c_rs, False, lambda copy: copy.wait_send())
     near_copies(d_source, d_recv, d_ss, d_rs, True, lambda copy: copy.wait_send())
-    for dt, dr in others:
-        c, k = lax.rem(t + dt, T), lax.rem(r + dr, RK)
-        remote(g_send, g_recv.at[me], g_ss.at[c * RK + k], g_rs.at[me], c, k).wait_send()
+    for copies in (
+        rank_copies(b_recv, b_all, b2_ss, b2_rs),
+        rank_copies(e_sum, e_all, e2_ss, e2_rs),
+        rank_copies(g_send, g_all, g_ss, g_rs),
+    ):
+        for copy in copies:
+            copy.wait_send()
 
 
 def fused(
@@ -600,7 +625,6 @@
     data_weight,
 ):
     T, RK = lax.axis_size("tile"), lax.axis_size("rank")
-    N = T * RK
     rows = direction.shape[0] // 128
     pr = rows // T
     NBS, KC = near_blocks.shape[0], near_blocks.shape[1]
@@ -643,34 +667,41 @@
             pltpu.VMEM((rows, 128), f32),
             pltpu.VMEM((rows, 128), f32),
             pltpu.VMEM((1, 128), f32),
-            pltpu.VMEM((N, 1, 128), f32),
+            pltpu.VMEM((T, 1, 128), f32),
+            pltpu.VMEM((RK, T, 1, 128), f32),
             pltpu.VMEM((3, RK, KG, 128), f32),
             pltpu.VMEM((3, RK, KG, 128), bf16),
             pltpu.VMEM((1 + 3 * RK, KG, 128), bf16),
             pltpu.VMEM((3, RK, KG, 128), bf16),
             pltpu.VMEM((T, 1, 128), f32),
-            pltpu.VMEM((N, 1, 128), f32),
+            pltpu.VMEM((T, 1, 128), f32),
+            pltpu.VMEM((1, 128), f32),
+            pltpu.VMEM((RK, 1, 128), f32),
             pltpu.VMEM((rows, 128), f32),
-            pltpu.VMEM((T, pr, 128), f32),
-            pltpu.VMEM((T, pr, 128), f32),
+            pltpu.VMEM((T, 2 * pr, 128), f32),
+            pltpu.VMEM((T, 2 * pr, 128), f32),
             pltpu.VMEM((1, 128), f32),
-            pltpu.VMEM((N, 1, 128), f32),
+            pltpu.VMEM((RK, 1, 128), f32),
             pltpu.VMEM((NBP, KC * LD), f32),
             sem((10,)),
             sem((T,)),
             sem((T,)),
-            sem((N,)),
-            sem((N,)),
+            sem((T,)),
+            sem((T,)),
+            sem((RK,)),
+            sem((RK,)),
             sem((3, RK)),
             sem((3, RK)),
             sem((3, RK)),
             sem((3, RK)),
-            sem((N,)),
-            sem((N,)),
             sem((T,)),
             sem((T,)),
-            sem((N,)),
-            sem((N,)),
+            sem((RK,)),
+            sem((RK,)),
+            sem((T,)),
+            sem((T,)),
+            sem((RK,)),
+            sem((RK,)),
         ],
         compiler_params=pltpu.CompilerParams(
             collective_id=0, has_side_effects=True, vmem_limit_bytes=64 * 1024 * 1024

time: 32.4 us -> 37.1 us (1.15)
  Pallas kernels: 29.5 us -> 34.2 us
    pallas_call x1, Pallas kernels: 29.5 us -> 34.2 us  [fused(): pl.pallas_call(functools.partial(cg_kernel, (T, RK, NBS, KC, WR)), out_sh...]
where the time goes in v3:
time: 37.1 us; the launch traced here: 36.9 us
  Pallas kernels  34.2 us (92%)
  other arithmetic  1.4 us (4%)
  between operations  1.29 us (3%)
    pallas_call x1, Pallas kernels, fused(): pl.pallas_call(functools.partial(cg_kernel, (T, RK, NBS, KC, WR)), out_sh...  34.2 us
    reshape x1, other arithmetic, fused(): x.reshape(-1)  1.4 us

profile of v3, /device:TPU:0, one launch (start us, length us, event | category | flops | bytes accessed | tf_op | source)
XLA Modules:
  0.0 36.9 jit_solution(6222355545291988649)
XLA Ops:
  1.3 34.2 %shard_map.139 = (f32[16,128]{1,0:T(8,128)}, f32[16,128]{1,0:T(8,128)}, f32[16,128]{1,0:T(8,128)}) custom-call(f32[16,128]{1,0:T(8,128)} %bitcast.28, f32[16,128]{1,0:T(8,128)} %bitcast.29, s32[16,128]{1,0:T(8,128)} %bitcast.30, bf16[64,2048]{1,0:T(8,128)(2,1)} %col_hbm.1, bf16[6,64,1024]{2,1,0:T(8,128)(2,1)} %bitcast.26, bf16[8,64,64]{2,1,0:T(8,128)(2,1)} %bitcast.27, ...), custom_call_target="tpu_custom_call" | custom-call | tf_op jit(solution)/shard_map/pallas_call | solution.py:644
  35.5 1.4 %add_bitcast_fusion = (f32[2048]{0:T(1024)}, f32[2048]{0:T(1024)}, f32[2048]{0:T(1024)}) fusion(f32[16,128]{1,0:T(8,128)} %get-tuple-element.8, f32[2048]{0:T(1024)} %param.14, f32[16,128]{1,0:T(8,128)} %get-tuple-element.6, f32[16,128]{1,0:T(8,128)} %get-tuple-element.7, f32[2048]{0:T(1024)} %param.13, f32[2048]{0:T(1024)} %param.12), kind=kLoop, calls=%fused_computation.2 | loop fusion | flops 12288 | bytes 73728 | tf_op jit(solution)/shard_map/reshape | solution.py:725

commit v4 on v2

--- a/solution.py
+++ b/solution.py
@@ -442,7 +442,6 @@
     weighted = (weight_s[...] * (far_s[...] + near)).astype(bf16)
     d_send[0] = weighted
     weighted_f[...] = weighted.astype(f32)
-    near_copies(d_source, d_recv, d_ss, d_rs, True, lambda copy: copy.start())
     d_recv[1, r] = weighted
 
     back_part = jnp.zeros((1, WR), f32)
@@ -464,6 +463,8 @@
                 remote(
                     e_send.at[c], e_recv.at[me], e_ss.at[c * RK + k], e_rs.at[me], c, k
                 ).start()
+
+    near_copies(d_source, d_recv, d_ss, d_rs, True, lambda copy: copy.start())
 
     near_waits(d_recv, d_ss, d_rs, True)
     chosen = []

time: 32.4 us -> 32.4 us (level)
  no operation moved by 1% of the time
where the time goes in v4:
time: 32.4 us; the launch traced here: 32.1 us
  Pallas kernels  29.5 us (91%)
  other arithmetic  1.4 us (4%)
  between operations  1.29 us (4%)
    pallas_call x1, Pallas kernels, fused(): pl.pallas_call(functools.partial(cg_kernel, (T, RK, NBS, KC, WR)), out_sh...  29.5 us
    reshape x1, other arithmetic, fused(): x.reshape(-1)  1.4 us

profile of v4, /device:TPU:0, one launch (start us, length us, event | category | flops | bytes accessed | tf_op | source)
XLA Modules:
  0.0 32.1 jit_solution(17533882681939715447)
XLA Ops:
  1.3 29.5 %shard_map.139 = (f32[16,128]{1,0:T(8,128)}, f32[16,128]{1,0:T(8,128)}, f32[16,128]{1,0:T(8,128)}) custom-call(f32[16,128]{1,0:T(8,128)} %bitcast.28, f32[16,128]{1,0:T(8,128)} %bitcast.29, s32[16,128]{1,0:T(8,128)} %bitcast.30, bf16[64,2048]{1,0:T(8,128)(2,1)} %col_hbm.1, bf16[6,64,1024]{2,1,0:T(8,128)(2,1)} %bitcast.26, bf16[8,64,64]{2,1,0:T(8,128)(2,1)} %bitcast.27, ...), custom_call_target="tpu_custom_call" | custom-call | tf_op jit(solution)/shard_map/pallas_call | solution.py:621
  30.7 1.4 %add_bitcast_fusion = (f32[2048]{0:T(1024)}, f32[2048]{0:T(1024)}, f32[2048]{0:T(1024)}) fusion(f32[16,128]{1,0:T(8,128)} %get-tuple-element.8, f32[2048]{0:T(1024)} %param.14, f32[16,128]{1,0:T(8,128)} %get-tuple-element.6, f32[16,128]{1,0:T(8,128)} %get-tuple-element.7, f32[2048]{0:T(1024)} %param.13, f32[2048]{0:T(1024)} %param.12), kind=kLoop, calls=%fused_computation.2 | loop fusion | flops 12288 | bytes 73728 | tf_op jit(solution)/shard_map/reshape | solution.py:695
